TPU v7x, 32 devices: a whole 2x2x4 slice. The times are simulated.
32 devices in a mesh: vocab: 8 (over z, y), section: 4 (over x, core).
Axes of the slice: x: 2, y: 2, z: 4, core: 2. Of those that a mesh axis runs over, the one named last changes fastest.
Arguments:
- hidden: bfloat16 [4, 32, 8192], P('section', 'vocab'), may hold values from -64 to 64
- policy_head: bfloat16 [9504, 8192], P(('vocab', 'section')), may hold values from -1 to 1
- reference_head: bfloat16 [9504, 8192], P(('vocab', 'section')), may hold values from -1 to 1
- targets: int32 [4, 32], replicated, may hold values from 0 to 9503
- loss_mask: int32 [4, 32], replicated, may hold values 0 or 1
Outputs:
- token_logprob: float32 [4, 32], replicated
- token_kl: float32 [4, 32], replicated
- totals: float32 [3], replicated
All inputs are finite; a program needn't handle non-finite values.
Results may differ from a plain program's by a relative error of at most 0.0003.
Values may be sent and summed in bfloat16 or wider, within the bound.
A program may use at most 128 MiB of HBM per device.

v0:
```python
import functools
import itertools

import jax
import jax.numpy as jnp
from jax import lax
from jax.experimental import pallas as pl
from jax.experimental.pallas import tpu as pltpu
from jax.sharding import PartitionSpec as P

MESH = pl.DeviceIdType.MESH


def split_axis(size):
    return (size // 2, 2) if size % 2 == 0 else (size, 1)


def power_of_two(size):
    return size & (size - 1) == 0


def flip(index, step, size):
    result = index
    bit = 1
    while bit < size:
        if step & bit:
            result = result + bit - 2 * bit * ((index // bit) % 2)
        bit *= 2
    return result


def target_of(index, step, size):
    if step == 0:
        return index
    return flip(index, step, size) if power_of_two(size) else (index + step) % size


def source_of(index, step, size):
    if step == 0:
        return index
    return flip(index, step, size) if power_of_two(size) else (index + size - step) % size


def merge(parts):
    tops = [part[0:1] for part in parts]
    rtops = [part[1:2] for part in parts]
    top = functools.reduce(jnp.maximum, tops)
    rtop = functools.reduce(jnp.maximum, rtops)
    total = first = cross = chosen = rtotal = 0.0
    for part in parts:
        shift = part[0:1] - top
        scale = jnp.exp(shift)
        total = total + scale * part[2:3]
        first = first + scale * (part[3:4] + shift * part[2:3])
        cross = cross + scale * part[4:5]
        chosen = chosen + part[5:6]
        rtotal = rtotal + jnp.exp(part[1:2] - rtop) * part[6:7]
    return top, rtop, total, first, cross, chosen, rtotal


def to_groups(values, A, B, piece):
    return jnp.concatenate(
        [
            values[m : m + 1, (i * B + j) * piece : (i * B + j + 1) * piece]
            for m in range(values.shape[0]) for j in range(B) for i in range(A)
        ],
        axis=1,
    )


def from_groups(values, micro, A, B, piece):
    starts = [((m * B + j) * A + i) * piece for m in range(micro) for i in range(A) for j in range(B)]
    return jnp.concatenate([values[:, at : at + piece] for at in starts], axis=1)


PARTS = 2
STEPS = 2


def kernel(
    sizes, hid, hp, hr, tgt, out,
    strip, rows, wp, wr, plog_acc, rlog_acc, plane, line,
    local_sem, strip_sent, strip_sem, rows_sent, core_sem, stat_sent, recv_sem, stat_sem,
):
    vocab, section = sizes
    A, B = split_axis(vocab)
    X, C = split_axis(section)
    v, s = lax.axis_index("vocab"), lax.axis_index("section")
    a, b = v // B, v % B
    x, c = s // C, s % C
    dims = (A, B, X, C)
    here = (a, b, x, c)
    piece, width = hid.shape[1], hid.shape[2]
    groups, high = rows.shape[0], rows.shape[1]
    tokens = groups * high
    count = wp.shape[0]
    share_width = width // PARTS
    step_width = share_width // STEPS
    bundle = 128 // high if tokens % 128 == 0 and 128 % high == 0 else groups
    tile = bundle * high

    def device(at):
        return (at[0] * B + at[1], at[2] * C + at[3])

    def group(at):
        return (at[2] * C + at[3]) * B + at[1]

    def to(step):
        return tuple(target_of(i, d, n) for i, d, n in zip(here, step, dims))

    def back(step):
        return tuple(source_of(i, d, n) for i, d, n in zip(here, step, dims))

    line_steps = [(d, 0, 0, 0) for d in range(1, A)]
    plane_steps = [(0,) + e for e in itertools.product(range(B), range(X), range(C)) if any(e)]
    barrier = pltpu.get_barrier_semaphore()
    for step in line_steps + plane_steps:
        pl.semaphore_signal(barrier, inc=1, device_id=device(to(step)), device_id_type=MESH)

    own = pltpu.make_async_copy(hid.at[0], strip.at[a], local_sem.at[0])
    own.start()
    load_p = pltpu.make_async_copy(hp, wp, local_sem.at[1])
    load_p.start()
    load_r = pltpu.make_async_copy(hr, wr, local_sem.at[2])
    load_r.start()
    plog_acc[...] = jnp.zeros_like(plog_acc)
    rlog_acc[...] = jnp.zeros_like(rlog_acc)
    wanted = to_groups(tgt[...], A, B, piece)
    own.wait()
    pl.semaphore_wait(barrier, len(line_steps) + len(plane_steps))

    keys = {}

    def view(at, h, half):
        lo, size = h * share_width, share_width
        if half is not None:
            size = share_width // 2
            lo = lo + half * size
        return rows.at[group(at), :, pl.ds(lo, size)]

    def describe(key, step, at, h, half):
        part = view(at, h, half)
        if key[0] == "core":
            arrived = core_sem.at[h]
        else:
            arrived = recv_sem.at[keys.setdefault((h,) + key, len(keys))]
        return pltpu.make_async_remote_copy(
            src_ref=part, dst_ref=part, send_sem=rows_sent.at[0], recv_sem=arrived,
            device_id=device(to(step)), device_id_type=MESH,
        )

    def copy(key, step, at, h, half=None):
        describe(key, step, at, h, half).start()

    def arrive(key, step, at, h, half=None):
        describe(key, step, at, h, half).wait_recv()

    def to_cores(step, h):
        for dc in range(1, C):
            copy(("core", step, dc), (0, 0, 0, dc), back(step), h)

    def send_strip(h):
        part = strip.at[a, :, pl.ds(h * share_width, share_width)]
        for step in line_steps:
            pltpu.make_async_remote_copy(
                src_ref=part, dst_ref=part, send_sem=strip_sent.at[0], recv_sem=strip_sem.at[h],
                device_id=device(to(step)), device_id_type=MESH,
            ).start()

    def fan(h):
        columns = pl.ds(h * share_width, share_width)
        if A > 1:
            part = strip.at[pl.ds(0, A - 1), :, columns]
            pltpu.make_async_copy(part, part, strip_sem.at[h]).wait()
        rows[group(here), :, columns] = jnp.concatenate(
            [strip[i, :, columns] for i in range(A)], axis=0
        )
        for dx in range(1, X):
            copy(("x", dx), (0, 0, dx, 0), here, h)
        for db in range(1, B):
            copy(("b", db), (0, db, 0, 0), here, h)
        to_cores((0, 0, 0, 0), h)

    def cross(h):
        for dx in range(1, X):
            at = back((0, 0, dx, 0))
            arrive(("x", dx), (0, 0, dx, 0), at, h)
            for db in range(1, B):
                copy(("xb", dx, db), (0, db, 0, 0), at, h, 0)
        for db in range(1, B):
            at = back((0, db, 0, 0))
            arrive(("b", db), (0, db, 0, 0), at, h)
            for dx in range(1, X):
                copy(("bx", dx, db), (0, 0, dx, 0), at, h, 1)
        for dx in range(1, X):
            to_cores((0, 0, dx, 0), h)
        for db in range(1, B):
            to_cores((0, db, 0, 0), h)

    def corner(h):
        for dx in range(1, X):
            for db in range(1, B):
                at = back((0, db, dx, 0))
                arrive(("xb", dx, db), (0, db, 0, 0), at, h, 0)
                arrive(("bx", dx, db), (0, 0, dx, 0), at, h, 1)
                to_cores((0, db, dx, 0), h)

    def from_cores(h):
        if C > 1:
            part = rows.at[pl.ds(0, groups // C * (C - 1)), :, pl.ds(0, share_width)]
            pltpu.make_async_copy(part, part, core_sem.at[h]).wait()

    dims_nt = (((1,), (1,)), ((), ()))

    def multiply(k):
        columns = pl.ds(k * step_width, step_width)

        def tile_of(n):
            mine = rows[pl.ds(n * bundle, bundle), :, columns].reshape(tile, step_width)
            place = pl.ds(n * tile if isinstance(n, int) else pl.multiple_of(n * tile, tile), tile)
            plog_acc[:, place] += lax.dot_general(
                wp[:, columns], mine, dims_nt, preferred_element_type=jnp.float32
            )
            rlog_acc[:, place] += lax.dot_general(
                wr[:, columns], mine, dims_nt, preferred_element_type=jnp.float32
            )

        if tokens == tile:
            tile_of(0)
        else:
            pl.loop(0, tokens // tile)(tile_of)

    for h in range(PARTS):
        send_strip(h)
    for u in range(PARTS + 1):
        if u < PARTS:
            fan(u)
        if 1 <= u:
            cross(u - 1)
        if 2 <= u:
            corner(u - 2)
    load_p.wait()
    load_r.wait()
    early = (PARTS - 1) * STEPS
    for k in range(early):
        if k % STEPS == 0:
            from_cores(k // STEPS)
        if k == early // 2:
            corner(PARTS - 1)
        multiply(k)
    if not early:
        corner(PARTS - 1)
    from_cores(PARTS - 1)
    for k in range(early, PARTS * STEPS):
        multiply(k)

    offset = (v * section + s) * count
    moments = []
    for n in range(tokens // tile):
        place = slice(n * tile, (n + 1) * tile)
        plog, rlog = plog_acc[:, place], rlog_acc[:, place]
        top = jnp.max(plog, axis=0, keepdims=True)
        shift = plog - top
        weight = jnp.exp(shift)
        total = jnp.sum(weight, axis=0, keepdims=True)
        first = jnp.sum(weight * shift, axis=0, keepdims=True)
        across = jnp.sum(weight * (plog - rlog), axis=0, keepdims=True)
        ids = offset + lax.broadcasted_iota(jnp.int32, plog.shape, 0)
        chosen = jnp.sum(jnp.where(ids == wanted[:, place], plog, 0.0), axis=0, keepdims=True)
        rtop = jnp.max(rlog, axis=0, keepdims=True)
        rtotal = jnp.sum(jnp.exp(rlog - rtop), axis=0, keepdims=True)
        moments.append(
            jnp.concatenate([top, rtop, total, first, across, chosen, rtotal, jnp.zeros_like(top)], axis=0)
        )
    index = b * (X * C) + x * C + c
    plane[index] = jnp.concatenate(moments, axis=1) if len(moments) > 1 else moments[0]

    shared = []

    def share(step, buffer, at, start):
        i = keys.setdefault(("stat", step), len(keys)) - gather_keys
        op = pltpu.make_async_remote_copy(
            src_ref=buffer.at[at], dst_ref=buffer.at[at],
            send_sem=stat_sent.at[i], recv_sem=stat_sem.at[i],
            device_id=device(to(step)), device_id_type=MESH,
        )
        if start:
            op.start()
            shared.append(op)
        else:
            op.wait_recv()

    def plane_index(at):
        return at[1] * (X * C) + at[2] * C + at[3]

    gather_keys = len(keys)
    for step in plane_steps:
        share(step, plane, plane_index(here), True)
    if A > 1:
        sent = strip.at[pl.ds(0, A - 1)]
        pltpu.make_async_copy(sent, sent, strip_sent.at[0]).wait()
    if groups > 1:
        sent = rows.at[pl.ds(0, groups - 1)]
        pltpu.make_async_copy(sent, sent, rows_sent.at[0]).wait()
    for step in plane_steps:
        share(step, plane, plane_index(back(step)), False)
    merged = merge([plane[i] for i in range(B * X * C)])
    line[a] = jnp.concatenate(list(merged) + [jnp.zeros_like(merged[0])], axis=0)
    for step in line_steps:
        share(step, line, a, True)
    for step in line_steps:
        share(step, line, back(step)[0], False)
    merged = merge([line[i] for i in range(A)])
    out[...] = jnp.concatenate(list(merged) + [jnp.zeros_like(merged[0])], axis=0)
    for op in shared:
        op.wait_send()


def finish(A, B, stats, msk, out_lp, out_kl, out_tot):
    micro, span = msk.shape
    ordered = from_groups(stats[...], micro, A, B, span // (A * B))
    top, rtop, total, first, across, chosen, rtotal = [ordered[i : i + 1, :] for i in range(7)]
    log_total = jnp.log(total)
    lse = top + log_total
    logprob = chosen - lse
    entropy = log_total - first / total
    divergence = across / total - lse + (rtop + jnp.log(rtotal))
    mask = jnp.concatenate([msk[i : i + 1, :] for i in range(micro)], axis=1).astype(jnp.float32)
    scale = 1.0 / (micro * span)
    out_tot[0] = jnp.sum(mask * logprob) * scale
    out_tot[1] = jnp.sum(mask * entropy) * scale
    out_tot[2] = jnp.sum(mask * divergence) * scale
    for i in range(micro):
        out_lp[i : i + 1, :] = logprob[:, i * span : (i + 1) * span]
        out_kl[i : i + 1, :] = divergence[:, i * span : (i + 1) * span]


def on_device(sizes, hidden, policy_head, reference_head, targets, loss_mask):
    vocab, section = sizes
    A, B = split_axis(vocab)
    X, C = split_axis(section)
    piece, width = hidden.shape[1], hidden.shape[2]
    tokens = targets.size
    gathers = (X - 1) + (B - 1) + 2 * (X - 1) * (B - 1)
    stats = (B * X * C - 1) + (A - 1)
    anywhere = pl.BlockSpec(memory_space=pl.ANY)
    vmem = pl.BlockSpec(memory_space=pltpu.VMEM)
    heads = policy_head.size + reference_head.size
    moments = pl.pallas_call(
        functools.partial(kernel, sizes),
        out_shape=jax.ShapeDtypeStruct((8, tokens), jnp.float32),
        in_specs=[anywhere, anywhere, anywhere, vmem],
        out_specs=vmem,
        scratch_shapes=[
            pltpu.VMEM((A, piece, width), hidden.dtype),
            pltpu.VMEM((B * X * C, A * piece, width), hidden.dtype),
            pltpu.VMEM(policy_head.shape, policy_head.dtype),
            pltpu.VMEM(reference_head.shape, reference_head.dtype),
            pltpu.VMEM((policy_head.shape[0], tokens), jnp.float32),
            pltpu.VMEM((reference_head.shape[0], tokens), jnp.float32),
            pltpu.VMEM((B * X * C, 8, tokens), jnp.float32),
            pltpu.VMEM((A, 8, tokens), jnp.float32),
            pltpu.SemaphoreType.DMA((3,)),
            pltpu.SemaphoreType.DMA((1,)),
            pltpu.SemaphoreType.DMA((PARTS,)),
            pltpu.SemaphoreType.DMA((1,)),
            pltpu.SemaphoreType.DMA((PARTS,)),
            pltpu.SemaphoreType.DMA((stats,)),
            pltpu.SemaphoreType.DMA((PARTS * gathers,)),
            pltpu.SemaphoreType.DMA((stats,)),
        ],
        compiler_params=pltpu.CompilerParams(
            collective_id=0, has_side_effects=True, vmem_limit_bytes=60 * 1024 * 1024
        ),
        cost_estimate=pl.CostEstimate(
            flops=2 * tokens * heads, bytes_accessed=2 * heads, transcendentals=3 * tokens * policy_head.shape[0]
        ),
    )(hidden, policy_head, reference_head, targets)
    return pl.pallas_call(
        functools.partial(finish, A, B),
        out_shape=(
            jax.ShapeDtypeStruct(targets.shape, jnp.float32),
            jax.ShapeDtypeStruct(targets.shape, jnp.float32),
            jax.ShapeDtypeStruct((3,), jnp.float32),
        ),
        in_specs=[vmem, vmem],
        out_specs=(vmem, vmem, pl.BlockSpec(memory_space=pltpu.SMEM)),
    )(moments, loss_mask)


def solution(mesh):
    placed = (
        P("section", "vocab", None),
        P(("vocab", "section"), None),
        P(("vocab", "section"), None),
        P(),
        P(),
    )
    sizes = (mesh.shape["vocab"], mesh.shape["section"])
    return jax.shard_map(
        functools.partial(on_device, sizes),
        mesh=mesh, in_specs=placed, out_specs=(P(), P(), P()), check_vma=False,
    )
```

profile of v0, /device:TPU:0, one launch (start us, length us, event | category | flops | bytes accessed | tf_op | source)
XLA Modules:
  0.0 35.3 jit_solution(651292520471654856)
XLA Ops:
  0.6 33.2 %shard_map.76.stats = f32[8,128]{1,0:T(8,128)} custom-call(bf16[1,4,8192]{2,1,0:T(4,128)(2,1)} %hid.1, bf16[297,8192]{1,0:T(8,128)(2,1)} %hp.1, bf16[297,8192]{1,0:T(8,128)(2,1)} %hr.1, s32[4,32]{1,0:T(4,128)} %tgt.1), custom_call_target="tpu_custom_call" | custom-call | flops 1245708288 | bytes 9732096 | tf_op jit(solution)/shard_map/pallas_call | solution.py:349
  33.8 1.5 %shard_map.77 = (f32[4,32]{1,0:T(4,128)}, f32[4,32]{1,0:T(4,128)}, f32[3]{0:T(128)}) custom-call(f32[8,128]{1,0:T(8,128)} %shard_map.76.stats, s32[4,32]{1,0:T(4,128)} %msk.1), custom_call_target="tpu_custom_call" | custom-call | tf_op jit(solution)/shard_map/pallas_call | solution.py:379
where the time goes:
time: 35.5 us; the launch traced here: 35.3 us
  Pallas kernels  34.6 us (97%)
  between operations  0.64 us (2%)
    pallas_call x1, Pallas kernels, on_device(): pl.pallas_call(functools.partial(kernel, sizes), out_shape=jax.ShapeDtype...  33.2 us
    pallas_call x1, Pallas kernels, on_device(): pl.pallas_call(functools.partial(finish, A, B), out_shape=(jax.ShapeDtype...  1.46 us

commit v1 on v0

--- a/solution.py
+++ b/solution.py
@@ -42,20 +42,9 @@
 
 
 def merge(parts):
-    tops = [part[0:1] for part in parts]
-    rtops = [part[1:2] for part in parts]
-    top = functools.reduce(jnp.maximum, tops)
-    rtop = functools.reduce(jnp.maximum, rtops)
-    total = first = cross = chosen = rtotal = 0.0
-    for part in parts:
-        shift = part[0:1] - top
-        scale = jnp.exp(shift)
-        total = total + scale * part[2:3]
-        first = first + scale * (part[3:4] + shift * part[2:3])
-        cross = cross + scale * part[4:5]
-        chosen = chosen + part[5:6]
-        rtotal = rtotal + jnp.exp(part[1:2] - rtop) * part[6:7]
-    return top, rtop, total, first, cross, chosen, rtotal
+    top = functools.reduce(jnp.maximum, [part[8:16] for part in parts])
+    total = sum(jnp.exp(part[8:16] - top) * part[0:8] for part in parts)
+    return total, top
 
 
 def to_groups(values, A, B, piece):
@@ -79,8 +68,8 @@
 
 def kernel(
     sizes, hid, hp, hr, tgt, out,
-    strip, rows, wp, wr, plog_acc, rlog_acc, plane, line,
-    local_sem, strip_sent, strip_sem, rows_sent, core_sem, stat_sent, recv_sem, stat_sem,
+    strip, rows, wp, wr, acc, plane, line,
+    local_sem, strip_sent, strip_sem, rows_sent, core_sem, recv_sem, stat_sent, stat_sem,
 ):
     vocab, section = sizes
     A, B = split_axis(vocab)
@@ -94,6 +83,7 @@
     groups, high = rows.shape[0], rows.shape[1]
     tokens = groups * high
     count = wp.shape[0]
+    whole = acc.shape[0] - count
     share_width = width // PARTS
     step_width = share_width // STEPS
     bundle = 128 // high if tokens % 128 == 0 and 128 % high == 0 else groups
@@ -119,12 +109,6 @@
 
     own = pltpu.make_async_copy(hid.at[0], strip.at[a], local_sem.at[0])
     own.start()
-    load_p = pltpu.make_async_copy(hp, wp, local_sem.at[1])
-    load_p.start()
-    load_r = pltpu.make_async_copy(hr, wr, local_sem.at[2])
-    load_r.start()
-    plog_acc[...] = jnp.zeros_like(plog_acc)
-    rlog_acc[...] = jnp.zeros_like(rlog_acc)
     wanted = to_groups(tgt[...], A, B, piece)
     own.wait()
     pl.semaphore_wait(barrier, len(line_steps) + len(plane_steps))
@@ -218,12 +202,14 @@
         def tile_of(n):
             mine = rows[pl.ds(n * bundle, bundle), :, columns].reshape(tile, step_width)
             place = pl.ds(n * tile if isinstance(n, int) else pl.multiple_of(n * tile, tile), tile)
-            plog_acc[:, place] += lax.dot_general(
-                wp[:, columns], mine, dims_nt, preferred_element_type=jnp.float32
+            heads = jnp.concatenate(
+                [wp[:, columns], jnp.zeros((whole - count, step_width), wp.dtype), wr[:, columns]], axis=0
             )
-            rlog_acc[:, place] += lax.dot_general(
-                wr[:, columns], mine, dims_nt, preferred_element_type=jnp.float32
-            )
+            logits = lax.dot_general(heads, mine, dims_nt, preferred_element_type=jnp.float32)
+            if k == 0:
+                acc[:, place] = logits
+            else:
+                acc[:, place] += logits
 
         if tokens == tile:
             tile_of(0)
@@ -232,6 +218,10 @@
 
     for h in range(PARTS):
         send_strip(h)
+    load_p = pltpu.make_async_copy(hp, wp, local_sem.at[1])
+    load_p.start()
+    load_r = pltpu.make_async_copy(hr, wr, local_sem.at[2])
+    load_r.start()
     for u in range(PARTS + 1):
         if u < PARTS:
             fan(u)
@@ -258,72 +248,65 @@
     moments = []
     for n in range(tokens // tile):
         place = slice(n * tile, (n + 1) * tile)
-        plog, rlog = plog_acc[:, place], rlog_acc[:, place]
+        plog, rlog = acc[0:count, place], acc[whole : whole + count, place]
         top = jnp.max(plog, axis=0, keepdims=True)
         shift = plog - top
         weight = jnp.exp(shift)
         total = jnp.sum(weight, axis=0, keepdims=True)
-        first = jnp.sum(weight * shift, axis=0, keepdims=True)
+        first = jnp.sum(weight * plog, axis=0, keepdims=True)
         across = jnp.sum(weight * (plog - rlog), axis=0, keepdims=True)
         ids = offset + lax.broadcasted_iota(jnp.int32, plog.shape, 0)
         chosen = jnp.sum(jnp.where(ids == wanted[:, place], plog, 0.0), axis=0, keepdims=True)
         rtop = jnp.max(rlog, axis=0, keepdims=True)
         rtotal = jnp.sum(jnp.exp(rlog - rtop), axis=0, keepdims=True)
+        none = jnp.zeros_like(top)
         moments.append(
-            jnp.concatenate([top, rtop, total, first, across, chosen, rtotal, jnp.zeros_like(top)], axis=0)
+            jnp.concatenate(
+                [total, first, across, rtotal, chosen, none, none, none]
+                + [top, top, top, rtop, none, none, none, none],
+                axis=0,
+            )
         )
     index = b * (X * C) + x * C + c
     plane[index] = jnp.concatenate(moments, axis=1) if len(moments) > 1 else moments[0]
 
-    shared = []
-
-    def share(step, buffer, at, start):
-        i = keys.setdefault(("stat", step), len(keys)) - gather_keys
-        op = pltpu.make_async_remote_copy(
-            src_ref=buffer.at[at], dst_ref=buffer.at[at],
-            send_sem=stat_sent.at[i], recv_sem=stat_sem.at[i],
-            device_id=device(to(step)), device_id_type=MESH,
-        )
-        if start:
-            op.start()
-            shared.append(op)
-        else:
-            op.wait_recv()
-
-    def plane_index(at):
-        return at[1] * (X * C) + at[2] * C + at[3]
-
-    gather_keys = len(keys)
-    for step in plane_steps:
-        share(step, plane, plane_index(here), True)
+    def exchange(i, steps, buffer, position):
+        part = buffer.at[position]
+        for step in steps:
+            pltpu.make_async_remote_copy(
+                src_ref=part, dst_ref=part, send_sem=stat_sent.at[i], recv_sem=stat_sem.at[i],
+                device_id=device(to(step)), device_id_type=MESH,
+            ).start()
+
+    def exchanged(i, steps, buffer, sem):
+        if steps:
+            part = buffer.at[pl.ds(0, len(steps))]
+            pltpu.make_async_copy(part, part, sem.at[i]).wait()
+
+    exchange(0, plane_steps, plane, index)
     if A > 1:
         sent = strip.at[pl.ds(0, A - 1)]
         pltpu.make_async_copy(sent, sent, strip_sent.at[0]).wait()
     if groups > 1:
         sent = rows.at[pl.ds(0, groups - 1)]
         pltpu.make_async_copy(sent, sent, rows_sent.at[0]).wait()
-    for step in plane_steps:
-        share(step, plane, plane_index(back(step)), False)
-    merged = merge([plane[i] for i in range(B * X * C)])
-    line[a] = jnp.concatenate(list(merged) + [jnp.zeros_like(merged[0])], axis=0)
-    for step in line_steps:
-        share(step, line, a, True)
-    for step in line_steps:
-        share(step, line, back(step)[0], False)
-    merged = merge([line[i] for i in range(A)])
-    out[...] = jnp.concatenate(list(merged) + [jnp.zeros_like(merged[0])], axis=0)
-    for op in shared:
-        op.wait_send()
+    exchanged(0, plane_steps, plane, stat_sem)
+    line[a] = jnp.concatenate(merge([plane[i] for i in range(B * X * C)]), axis=0)
+    exchange(1, line_steps, line, a)
+    exchanged(0, plane_steps, plane, stat_sent)
+    exchanged(1, line_steps, line, stat_sem)
+    total, top = merge([line[i] for i in range(A)])
+    out[...] = jnp.concatenate([total[0:5], top[0:1], top[3:4], total[7:8]], axis=0)
+    exchanged(1, line_steps, line, stat_sent)
 
 
 def finish(A, B, stats, msk, out_lp, out_kl, out_tot):
     micro, span = msk.shape
     ordered = from_groups(stats[...], micro, A, B, span // (A * B))
-    top, rtop, total, first, across, chosen, rtotal = [ordered[i : i + 1, :] for i in range(7)]
-    log_total = jnp.log(total)
-    lse = top + log_total
+    total, first, across, rtotal, chosen, top, rtop = [ordered[i : i + 1, :] for i in range(7)]
+    lse = top + jnp.log(total)
     logprob = chosen - lse
-    entropy = log_total - first / total
+    entropy = lse - first / total
     divergence = across / total - lse + (rtop + jnp.log(rtotal))
     mask = jnp.concatenate([msk[i : i + 1, :] for i in range(micro)], axis=1).astype(jnp.float32)
     scale = 1.0 / (micro * span)
@@ -342,7 +325,6 @@
     piece, width = hidden.shape[1], hidden.shape[2]
     tokens = targets.size
     gathers = (X - 1) + (B - 1) + 2 * (X - 1) * (B - 1)
-    stats = (B * X * C - 1) + (A - 1)
     anywhere = pl.BlockSpec(memory_space=pl.ANY)
     vmem = pl.BlockSpec(memory_space=pltpu.VMEM)
     heads = policy_head.size + reference_head.size
@@ -356,18 +338,17 @@
             pltpu.VMEM((B * X * C, A * piece, width), hidden.dtype),
             pltpu.VMEM(policy_head.shape, policy_head.dtype),
             pltpu.VMEM(reference_head.shape, reference_head.dtype),
-            pltpu.VMEM((policy_head.shape[0], tokens), jnp.float32),
-            pltpu.VMEM((reference_head.shape[0], tokens), jnp.float32),
-            pltpu.VMEM((B * X * C, 8, tokens), jnp.float32),
-            pltpu.VMEM((A, 8, tokens), jnp.float32),
+            pltpu.VMEM((-(-policy_head.shape[0] // 16) * 16 + reference_head.shape[0], tokens), jnp.float32),
+            pltpu.VMEM((B * X * C, 16, tokens), jnp.float32),
+            pltpu.VMEM((A, 16, tokens), jnp.float32),
             pltpu.SemaphoreType.DMA((3,)),
             pltpu.SemaphoreType.DMA((1,)),
             pltpu.SemaphoreType.DMA((PARTS,)),
             pltpu.SemaphoreType.DMA((1,)),
             pltpu.SemaphoreType.DMA((PARTS,)),
-            pltpu.SemaphoreType.DMA((stats,)),
             pltpu.SemaphoreType.DMA((PARTS * gathers,)),
-            pltpu.SemaphoreType.DMA((stats,)),
+            pltpu.SemaphoreType.DMA((2,)),
+            pltpu.SemaphoreType.DMA((2,)),
         ],
         compiler_params=pltpu.CompilerParams(
             collective_id=0, has_side_effects=True, vmem_limit_bytes=60 * 1024 * 1024

time: 35.5 us -> 37.7 us (1.062)
  Pallas kernels: 34.6 us -> 36.9 us
    pallas_call x1, Pallas kernels: 33.2 us -> 35.4 us  [on_device(): pl.pallas_call(functools.partial(kernel, sizes), out_shape=jax.ShapeDtype...]
where the time goes in v1:
time: 37.7 us; the launch traced here: 37.5 us
  Pallas kernels  36.9 us (98%)
  between operations  0.64 us (2%)
    pallas_call x1, Pallas kernels, on_device(): pl.pallas_call(functools.partial(kernel, sizes), out_shape=jax.ShapeDtype...  35.4 us
    pallas_call x1, Pallas kernels, on_device(): pl.pallas_call(functools.partial(finish, A, B), out_shape=(jax.ShapeDtype...  1.46 us

profile of v1, /device:TPU:0, one launch (start us, length us, event | category | flops | bytes accessed | tf_op | source)
XLA Modules:
  0.0 37.5 jit_solution(7137159682410263604)
XLA Ops:
  0.6 35.4 %shard_map.76.stats = f32[8,128]{1,0:T(8,128)} custom-call(bf16[1,4,8192]{2,1,0:T(4,128)(2,1)} %hid.1, bf16[297,8192]{1,0:T(8,128)(2,1)} %hp.1, bf16[297,8192]{1,0:T(8,128)(2,1)} %hr.1, s32[4,32]{1,0:T(4,128)} %tgt.1), custom_call_target="tpu_custom_call" | custom-call | flops 1245708288 | bytes 9732096 | tf_op jit(solution)/shard_map/pallas_call | solution.py:331
  36.0 1.5 %shard_map.77 = (f32[4,32]{1,0:T(4,128)}, f32[4,32]{1,0:T(4,128)}, f32[3]{0:T(128)}) custom-call(f32[8,128]{1,0:T(8,128)} %shard_map.76.stats, s32[4,32]{1,0:T(4,128)} %msk.1), custom_call_target="tpu_custom_call" | custom-call | tf_op jit(solution)/shard_map/pallas_call | solution.py:360

commit v2 on v1

--- a/solution.py
+++ b/solution.py
@@ -68,7 +68,7 @@
 
 def kernel(
     sizes, hid, hp, hr, tgt, out,
-    strip, rows, wp, wr, acc, plane, line,
+    strip, rows, wp, wr, plog_acc, rlog_acc, plane, line,
     local_sem, strip_sent, strip_sem, rows_sent, core_sem, recv_sem, stat_sent, stat_sem,
 ):
     vocab, section = sizes
@@ -83,7 +83,6 @@
     groups, high = rows.shape[0], rows.shape[1]
     tokens = groups * high
     count = wp.shape[0]
-    whole = acc.shape[0] - count
     share_width = width // PARTS
     step_width = share_width // STEPS
     bundle = 128 // high if tokens % 128 == 0 and 128 % high == 0 else groups
@@ -109,6 +108,10 @@
 
     own = pltpu.make_async_copy(hid.at[0], strip.at[a], local_sem.at[0])
     own.start()
+    load_p = pltpu.make_async_copy(hp, wp, local_sem.at[1])
+    load_p.start()
+    load_r = pltpu.make_async_copy(hr, wr, local_sem.at[2])
+    load_r.start()
     wanted = to_groups(tgt[...], A, B, piece)
     own.wait()
     pl.semaphore_wait(barrier, len(line_steps) + len(plane_steps))
@@ -202,14 +205,14 @@
         def tile_of(n):
             mine = rows[pl.ds(n * bundle, bundle), :, columns].reshape(tile, step_width)
             place = pl.ds(n * tile if isinstance(n, int) else pl.multiple_of(n * tile, tile), tile)
-            heads = jnp.concatenate(
-                [wp[:, columns], jnp.zeros((whole - count, step_width), wp.dtype), wr[:, columns]], axis=0
-            )
-            logits = lax.dot_general(heads, mine, dims_nt, preferred_element_type=jnp.float32)
-            if k == 0:
-                acc[:, place] = logits
-            else:
-                acc[:, place] += logits
+            for head, total in ((wp, plog_acc), (wr, rlog_acc)):
+                logits = lax.dot_general(
+                    head[:, columns], mine, dims_nt, preferred_element_type=jnp.float32
+                )
+                if k == 0:
+                    total[:, place] = logits
+                else:
+                    total[:, place] += logits
 
         if tokens == tile:
             tile_of(0)
@@ -218,10 +221,6 @@
 
     for h in range(PARTS):
         send_strip(h)
-    load_p = pltpu.make_async_copy(hp, wp, local_sem.at[1])
-    load_p.start()
-    load_r = pltpu.make_async_copy(hr, wr, local_sem.at[2])
-    load_r.start()
     for u in range(PARTS + 1):
         if u < PARTS:
             fan(u)
@@ -231,24 +230,17 @@
             corner(u - 2)
     load_p.wait()
     load_r.wait()
-    early = (PARTS - 1) * STEPS
-    for k in range(early):
+    corner(PARTS - 1)
+    for k in range(PARTS * STEPS):
         if k % STEPS == 0:
             from_cores(k // STEPS)
-        if k == early // 2:
-            corner(PARTS - 1)
-        multiply(k)
-    if not early:
-        corner(PARTS - 1)
-    from_cores(PARTS - 1)
-    for k in range(early, PARTS * STEPS):
         multiply(k)
 
     offset = (v * section + s) * count
     moments = []
     for n in range(tokens // tile):
         place = slice(n * tile, (n + 1) * tile)
-        plog, rlog = acc[0:count, place], acc[whole : whole + count, place]
+        plog, rlog = plog_acc[:, place], rlog_acc[:, place]
         top = jnp.max(plog, axis=0, keepdims=True)
         shift = plog - top
         weight = jnp.exp(shift)
@@ -338,7 +330,8 @@
             pltpu.VMEM((B * X * C, A * piece, width), hidden.dtype),
             pltpu.VMEM(policy_head.shape, policy_head.dtype),
             pltpu.VMEM(reference_head.shape, reference_head.dtype),
-            pltpu.VMEM((-(-policy_head.shape[0] // 16) * 16 + reference_head.shape[0], tokens), jnp.float32),
+            pltpu.VMEM((policy_head.shape[0], tokens), jnp.float32),
+            pltpu.VMEM((reference_head.shape[0], tokens), jnp.float32),
             pltpu.VMEM((B * X * C, 16, tokens), jnp.float32),
             pltpu.VMEM((A, 16, tokens), jnp.float32),
             pltpu.SemaphoreType.DMA((3,)),

time: 37.7 us -> 36.2 us (0.960)
  Pallas kernels: 36.9 us -> 35.3 us
    pallas_call x1, Pallas kernels: 35.4 us -> 33.9 us  [on_device(): pl.pallas_call(functools.partial(kernel, sizes), out_shape=jax.ShapeDtype...]
where the time goes in v2:
time: 36.2 us; the launch traced here: 36 us
  Pallas kernels  35.3 us (98%)
  between operations  0.64 us (2%)
    pallas_call x1, Pallas kernels, on_device(): pl.pallas_call(functools.partial(kernel, sizes), out_shape=jax.ShapeDtype...  33.9 us
    pallas_call x1, Pallas kernels, on_device(): pl.pallas_call(functools.partial(finish, A, B), out_shape=(jax.ShapeDtype...  1.46 us

profile of v2, /device:TPU:0, one launch (start us, length us, event | category | flops | bytes accessed | tf_op | source)
XLA Modules:
  0.0 36.0 jit_solution(17984093904180386843)
XLA Ops:
  0.6 33.9 %shard_map.76.stats = f32[8,128]{1,0:T(8,128)} custom-call(bf16[1,4,8192]{2,1,0:T(4,128)(2,1)} %hid.1, bf16[297,8192]{1,0:T(8,128)(2,1)} %hp.1, bf16[297,8192]{1,0:T(8,128)(2,1)} %hr.1, s32[4,32]{1,0:T(4,128)} %tgt.1), custom_call_target="tpu_custom_call" | custom-call | flops 1245708288 | bytes 9732096 | tf_op jit(solution)/shard_map/pallas_call | solution.py:323
  34.5 1.5 %shard_map.77 = (f32[4,32]{1,0:T(4,128)}, f32[4,32]{1,0:T(4,128)}, f32[3]{0:T(128)}) custom-call(f32[8,128]{1,0:T(8,128)} %shard_map.76.stats, s32[4,32]{1,0:T(4,128)} %msk.1), custom_call_target="tpu_custom_call" | custom-call | tf_op jit(solution)/shard_map/pallas_call | solution.py:353

commit v3 on v2

--- a/solution.py
+++ b/solution.py
@@ -62,8 +62,8 @@
     return jnp.concatenate([values[:, at : at + piece] for at in starts], axis=1)
 
 
-PARTS = 2
-STEPS = 2
+PARTS = 4
+STEPS = 1
 
 
 def kernel(
@@ -230,8 +230,10 @@
             corner(u - 2)
     load_p.wait()
     load_r.wait()
-    corner(PARTS - 1)
+    early = (PARTS - 1) * STEPS
     for k in range(PARTS * STEPS):
+        if k == (early + 1) // 2:
+            corner(PARTS - 1)
         if k % STEPS == 0:
             from_cores(k // STEPS)
         multiply(k)

time: 36.2 us -> 36.4 us (level)
  no operation moved by 1% of the time
where the time goes in v3:
time: 36.4 us; the launch traced here: 36.2 us
  Pallas kernels  35.5 us (98%)
  between operations  0.64 us (2%)
    pallas_call x1, Pallas kernels, on_device(): pl.pallas_call(functools.partial(kernel, sizes), out_shape=jax.ShapeDtype...  34.1 us
    pallas_call x1, Pallas kernels, on_device(): pl.pallas_call(functools.partial(finish, A, B), out_shape=(jax.ShapeDtype...  1.46 us

profile of v3, /device:TPU:0, one launch (start us, length us, event | category | flops | bytes accessed | tf_op | source)
XLA Modules:
  0.0 36.2 jit_solution(9934480410271840567)
XLA Ops:
  0.6 34.1 %shard_map.76.stats = f32[8,128]{1,0:T(8,128)} custom-call(bf16[1,4,8192]{2,1,0:T(4,128)(2,1)} %hid.1, bf16[297,8192]{1,0:T(8,128)(2,1)} %hp.1, bf16[297,8192]{1,0:T(8,128)(2,1)} %hr.1, s32[4,32]{1,0:T(4,128)} %tgt.1), custom_call_target="tpu_custom_call" | custom-call | flops 1245708288 | bytes 9732096 | tf_op jit(solution)/shard_map/pallas_call | solution.py:325
  34.7 1.5 %shard_map.77 = (f32[4,32]{1,0:T(4,128)}, f32[4,32]{1,0:T(4,128)}, f32[3]{0:T(128)}) custom-call(f32[8,128]{1,0:T(8,128)} %shard_map.76.stats, s32[4,32]{1,0:T(4,128)} %msk.1), custom_call_target="tpu_custom_call" | custom-call | tf_op jit(solution)/shard_map/pallas_call | solution.py:355

commit v4 on v3

--- a/solution.py
+++ b/solution.py
@@ -41,10 +41,17 @@
     return flip(index, step, size) if power_of_two(size) else (index + size - step) % size
 
 
-def merge(parts):
-    top = functools.reduce(jnp.maximum, [part[8:16] for part in parts])
-    total = sum(jnp.exp(part[8:16] - top) * part[0:8] for part in parts)
-    return total, top
+def merge(buffer):
+    parts = range(buffer.shape[0])
+    top = functools.reduce(jnp.maximum, [buffer[i, 5:6, :] for i in parts])
+    rtop = functools.reduce(jnp.maximum, [buffer[i, 6:7, :] for i in parts])
+    row = lax.broadcasted_iota(jnp.int32, buffer.shape[1:], 0)
+    total = jnp.zeros(buffer.shape[1:], buffer.dtype)
+    for i in parts:
+        shift = jnp.where(row == 3, buffer[i, 6:7, :] - rtop, 0.0)
+        shift = jnp.where(row < 3, buffer[i, 5:6, :] - top, shift)
+        total = total + jnp.exp(shift) * buffer[i]
+    return jnp.where(row == 5, top, jnp.where(row == 6, rtop, total))
 
 
 def to_groups(values, A, B, piece):
@@ -62,8 +69,8 @@
     return jnp.concatenate([values[:, at : at + piece] for at in starts], axis=1)
 
 
-PARTS = 4
-STEPS = 1
+PARTS = 2
+STEPS = 2
 
 
 def kernel(
@@ -100,20 +107,18 @@
     def back(step):
         return tuple(source_of(i, d, n) for i, d, n in zip(here, step, dims))
 
+    own = pltpu.make_async_copy(hid.at[0], strip.at[a], local_sem.at[0])
+    own.start()
     line_steps = [(d, 0, 0, 0) for d in range(1, A)]
     plane_steps = [(0,) + e for e in itertools.product(range(B), range(X), range(C)) if any(e)]
     barrier = pltpu.get_barrier_semaphore()
     for step in line_steps + plane_steps:
         pl.semaphore_signal(barrier, inc=1, device_id=device(to(step)), device_id_type=MESH)
 
-    own = pltpu.make_async_copy(hid.at[0], strip.at[a], local_sem.at[0])
-    own.start()
     load_p = pltpu.make_async_copy(hp, wp, local_sem.at[1])
     load_p.start()
     load_r = pltpu.make_async_copy(hr, wr, local_sem.at[2])
     load_r.start()
-    wanted = to_groups(tgt[...], A, B, piece)
-    own.wait()
     pl.semaphore_wait(barrier, len(line_steps) + len(plane_steps))
 
     keys = {}
@@ -147,10 +152,10 @@
             copy(("core", step, dc), (0, 0, 0, dc), back(step), h)
 
     def send_strip(h):
-        part = strip.at[a, :, pl.ds(h * share_width, share_width)]
+        columns = pl.ds(h * share_width, share_width)
         for step in line_steps:
             pltpu.make_async_remote_copy(
-                src_ref=part, dst_ref=part, send_sem=strip_sent.at[0], recv_sem=strip_sem.at[h],
+                src_ref=hid.at[0, :, columns], dst_ref=strip.at[a, :, columns], send_sem=strip_sent.at[0], recv_sem=strip_sem.at[h],
                 device_id=device(to(step)), device_id_type=MESH,
             ).start()
 
@@ -221,6 +226,8 @@
 
     for h in range(PARTS):
         send_strip(h)
+    wanted = to_groups(tgt[...], A, B, piece)
+    own.wait()
     for u in range(PARTS + 1):
         if u < PARTS:
             fan(u)
@@ -256,9 +263,7 @@
         none = jnp.zeros_like(top)
         moments.append(
             jnp.concatenate(
-                [total, first, across, rtotal, chosen, none, none, none]
-                + [top, top, top, rtop, none, none, none, none],
-                axis=0,
+                [total, first, across, rtotal, chosen, top, rtop, none], axis=0
             )
         )
     index = b * (X * C) + x * C + c
@@ -285,12 +290,11 @@
         sent = rows.at[pl.ds(0, groups - 1)]
         pltpu.make_async_copy(sent, sent, rows_sent.at[0]).wait()
     exchanged(0, plane_steps, plane, stat_sem)
-    line[a] = jnp.concatenate(merge([plane[i] for i in range(B * X * C)]), axis=0)
+    line[a] = merge(plane)
     exchange(1, line_steps, line, a)
     exchanged(0, plane_steps, plane, stat_sent)
     exchanged(1, line_steps, line, stat_sem)
-    total, top = merge([line[i] for i in range(A)])
-    out[...] = jnp.concatenate([total[0:5], top[0:1], top[3:4], total[7:8]], axis=0)
+    out[...] = merge(line)
     exchanged(1, line_steps, line, stat_sent)
 
 
@@ -334,8 +338,8 @@
             pltpu.VMEM(reference_head.shape, reference_head.dtype),
             pltpu.VMEM((policy_head.shape[0], tokens), jnp.float32),
             pltpu.VMEM((reference_head.shape[0], tokens), jnp.float32),
-            pltpu.VMEM((B * X * C, 16, tokens), jnp.float32),
-            pltpu.VMEM((A, 16, tokens), jnp.float32),
+            pltpu.VMEM((B * X * C, 8, tokens), jnp.float32),
+            pltpu.VMEM((A, 8, tokens), jnp.float32),
             pltpu.SemaphoreType.DMA((3,)),
             pltpu.SemaphoreType.DMA((1,)),
             pltpu.SemaphoreType.DMA((PARTS,)),

time: 36.4 us -> 35.6 us (0.978)
  Pallas kernels: 35.5 us -> 34.7 us
    pallas_call x1, Pallas kernels: 34.1 us -> 33.2 us  [on_device(): pl.pallas_call(functools.partial(kernel, sizes), out_shape=jax.ShapeDtype...]
where the time goes in v4:
time: 35.6 us; the launch traced here: 35.3 us
  Pallas kernels  34.7 us (97%)
  between operations  0.64 us (2%)
    pallas_call x1, Pallas kernels, on_device(): pl.pallas_call(functools.partial(kernel, sizes), out_shape=jax.ShapeDtype...  33.2 us
    pallas_call x1, Pallas kernels, on_device(): pl.pallas_call(functools.partial(finish, A, B), out_shape=(jax.ShapeDtype...  1.46 us

profile of v4, /device:TPU:0, one launch (start us, length us, event | category | flops | bytes accessed | tf_op | source)
XLA Modules:
  0.0 35.3 jit_solution(4798604192749077988)
XLA Ops:
  0.6 33.2 %shard_map.76.stats = f32[8,128]{1,0:T(8,128)} custom-call(bf16[1,4,8192]{2,1,0:T(4,128)(2,1)} %hid.1, bf16[297,8192]{1,0:T(8,128)(2,1)} %hp.1, bf16[297,8192]{1,0:T(8,128)(2,1)} %hr.1, s32[4,32]{1,0:T(4,128)} %tgt.1), custom_call_target="tpu_custom_call" | custom-call | flops 1245708288 | bytes 9732096 | tf_op jit(solution)/shard_map/pallas_call | solution.py:329
  33.9 1.5 %shard_map.77 = (f32[4,32]{1,0:T(4,128)}, f32[4,32]{1,0:T(4,128)}, f32[3]{0:T(128)}) custom-call(f32[8,128]{1,0:T(8,128)} %shard_map.76.stats, s32[4,32]{1,0:T(4,128)} %msk.1), custom_call_target="tpu_custom_call" | custom-call | tf_op jit(solution)/shard_map/pallas_call | solution.py:359

commit v5 on v4

--- a/solution.py
+++ b/solution.py
@@ -24,7 +24,7 @@
     bit = 1
     while bit < size:
         if step & bit:
-            result = result + bit - 2 * bit * ((index // bit) % 2)
+            result = result + bit - 2 * bit * lax.rem(lax.div(index, bit), 2)
         bit *= 2
     return result
 
@@ -32,13 +32,13 @@
 def target_of(index, step, size):
     if step == 0:
         return index
-    return flip(index, step, size) if power_of_two(size) else (index + step) % size
+    return flip(index, step, size) if power_of_two(size) else lax.rem(index + step, size)
 
 
 def source_of(index, step, size):
     if step == 0:
         return index
-    return flip(index, step, size) if power_of_two(size) else (index + size - step) % size
+    return flip(index, step, size) if power_of_two(size) else lax.rem(index + size - step, size)
 
 
 def merge(buffer):
@@ -69,8 +69,8 @@
     return jnp.concatenate([values[:, at : at + piece] for at in starts], axis=1)
 
 
-PARTS = 2
-STEPS = 2
+PARTS = 4
+STEPS = 1
 
 
 def kernel(
@@ -82,8 +82,8 @@
     A, B = split_axis(vocab)
     X, C = split_axis(section)
     v, s = lax.axis_index("vocab"), lax.axis_index("section")
-    a, b = v // B, v % B
-    x, c = s // C, s % C
+    a, b = lax.div(v, B), lax.rem(v, B)
+    x, c = lax.div(s, C), lax.rem(s, C)
     dims = (A, B, X, C)
     here = (a, b, x, c)
     piece, width = hid.shape[1], hid.shape[2]
@@ -101,11 +101,14 @@
     def group(at):
         return (at[2] * C + at[3]) * B + at[1]
 
+    outward = [[target_of(i, d, n) for d in range(n)] for i, n in zip(here, dims)]
+    inward = [[source_of(i, d, n) for d in range(n)] for i, n in zip(here, dims)]
+
     def to(step):
-        return tuple(target_of(i, d, n) for i, d, n in zip(here, step, dims))
+        return tuple(known[d] for known, d in zip(outward, step))
 
     def back(step):
-        return tuple(source_of(i, d, n) for i, d, n in zip(here, step, dims))
+        return tuple(known[d] for known, d in zip(inward, step))
 
     own = pltpu.make_async_copy(hid.at[0], strip.at[a], local_sem.at[0])
     own.start()
@@ -132,10 +135,7 @@
 
     def describe(key, step, at, h, half):
         part = view(at, h, half)
-        if key[0] == "core":
-            arrived = core_sem.at[h]
-        else:
-            arrived = recv_sem.at[keys.setdefault((h,) + key, len(keys))]
+        arrived = recv_sem.at[keys.setdefault((h,) + key, len(keys))]
         return pltpu.make_async_remote_copy(
             src_ref=part, dst_ref=part, send_sem=rows_sent.at[0], recv_sem=arrived,
             device_id=device(to(step)), device_id_type=MESH,
@@ -147,9 +147,14 @@
     def arrive(key, step, at, h, half=None):
         describe(key, step, at, h, half).wait_recv()
 
-    def to_cores(step, h):
+    def to_cores(dx, h):
+        first = (back((0, 0, dx, 0))[2] * C + c) * B
+        part = rows.at[pl.ds(first, B), :, pl.ds(h * share_width, share_width)]
         for dc in range(1, C):
-            copy(("core", step, dc), (0, 0, 0, dc), back(step), h)
+            pltpu.make_async_remote_copy(
+                src_ref=part, dst_ref=part, send_sem=rows_sent.at[0], recv_sem=core_sem.at[h],
+                device_id=device(to((0, 0, 0, dc))), device_id_type=MESH,
+            ).start()
 
     def send_strip(h):
         columns = pl.ds(h * share_width, share_width)
@@ -171,7 +176,6 @@
             copy(("x", dx), (0, 0, dx, 0), here, h)
         for db in range(1, B):
             copy(("b", db), (0, db, 0, 0), here, h)
-        to_cores((0, 0, 0, 0), h)
 
     def cross(h):
         for dx in range(1, X):
@@ -184,10 +188,7 @@
             arrive(("b", db), (0, db, 0, 0), at, h)
             for dx in range(1, X):
                 copy(("bx", dx, db), (0, 0, dx, 0), at, h, 1)
-        for dx in range(1, X):
-            to_cores((0, 0, dx, 0), h)
-        for db in range(1, B):
-            to_cores((0, db, 0, 0), h)
+        to_cores(0, h)
 
     def corner(h):
         for dx in range(1, X):
@@ -195,7 +196,7 @@
                 at = back((0, db, dx, 0))
                 arrive(("xb", dx, db), (0, db, 0, 0), at, h, 0)
                 arrive(("bx", dx, db), (0, 0, dx, 0), at, h, 1)
-                to_cores((0, db, dx, 0), h)
+            to_cores(dx, h)
 
     def from_cores(h):
         if C > 1:

time: 35.6 us -> 36.3 us (1.020)
  Pallas kernels: 34.7 us -> 35.4 us
    pallas_call x1, Pallas kernels: 33.2 us -> 33.9 us  [on_device(): pl.pallas_call(functools.partial(kernel, sizes), out_shape=jax.ShapeDtype...]
where the time goes in v5:
time: 36.3 us; the launch traced here: 36 us
  Pallas kernels  35.4 us (98%)
  between operations  0.64 us (2%)
    pallas_call x1, Pallas kernels, on_device(): pl.pallas_call(functools.partial(kernel, sizes), out_shape=jax.ShapeDtype...  33.9 us
    pallas_call x1, Pallas kernels, on_device(): pl.pallas_call(functools.partial(finish, A, B), out_shape=(jax.ShapeDtype...  1.46 us

profile of v5, /device:TPU:0, one launch (start us, length us, event | category | flops | bytes accessed | tf_op | source)
XLA Modules:
  0.0 36.0 jit_solution(2154841136322043384)
XLA Ops:
  0.6 33.9 %shard_map.76.stats = f32[8,128]{1,0:T(8,128)} custom-call(bf16[1,4,8192]{2,1,0:T(4,128)(2,1)} %hid.1, bf16[297,8192]{1,0:T(8,128)(2,1)} %hp.1, bf16[297,8192]{1,0:T(8,128)(2,1)} %hr.1, s32[4,32]{1,0:T(4,128)} %tgt.1), custom_call_target="tpu_custom_call" | custom-call | flops 1245708288 | bytes 9732096 | tf_op jit(solution)/shard_map/pallas_call | solution.py:330
  34.6 1.5 %shard_map.77 = (f32[4,32]{1,0:T(4,128)}, f32[4,32]{1,0:T(4,128)}, f32[3]{0:T(128)}) custom-call(f32[8,128]{1,0:T(8,128)} %shard_map.76.stats, s32[4,32]{1,0:T(4,128)} %msk.1), custom_call_target="tpu_custom_call" | custom-call | tf_op jit(solution)/shard_map/pallas_call | solution.py:360

commit v6 on v5

--- a/solution.py
+++ b/solution.py
@@ -69,8 +69,8 @@
     return jnp.concatenate([values[:, at : at + piece] for at in starts], axis=1)
 
 
-PARTS = 4
-STEPS = 1
+PARTS = 2
+STEPS = 2
 
 
 def kernel(

time: 36.3 us -> 35.9 us (0.989)
  no operation moved by 1% of the time
where the time goes in v6:
time: 35.9 us; the launch traced here: 35.7 us
  Pallas kernels  35.1 us (98%)
  between operations  0.64 us (2%)
    pallas_call x1, Pallas kernels, on_device(): pl.pallas_call(functools.partial(kernel, sizes), out_shape=jax.ShapeDtype...  33.6 us
    pallas_call x1, Pallas kernels, on_device(): pl.pallas_call(functools.partial(finish, A, B), out_shape=(jax.ShapeDtype...  1.46 us

profile of v6, /device:TPU:0, one launch (start us, length us, event | category | flops | bytes accessed | tf_op | source)
XLA Modules:
  0.0 35.7 jit_solution(9047232239355400378)
XLA Ops:
  0.6 33.6 %shard_map.76.stats = f32[8,128]{1,0:T(8,128)} custom-call(bf16[1,4,8192]{2,1,0:T(4,128)(2,1)} %hid.1, bf16[297,8192]{1,0:T(8,128)(2,1)} %hp.1, bf16[297,8192]{1,0:T(8,128)(2,1)} %hr.1, s32[4,32]{1,0:T(4,128)} %tgt.1), custom_call_target="tpu_custom_call" | custom-call | flops 1245708288 | bytes 9732096 | tf_op jit(solution)/shard_map/pallas_call | solution.py:330
  34.2 1.5 %shard_map.77 = (f32[4,32]{1,0:T(4,128)}, f32[4,32]{1,0:T(4,128)}, f32[3]{0:T(128)}) custom-call(f32[8,128]{1,0:T(8,128)} %shard_map.76.stats, s32[4,32]{1,0:T(4,128)} %msk.1), custom_call_target="tpu_custom_call" | custom-call | tf_op jit(solution)/shard_map/pallas_call | solution.py:360
